TPU v7x, 32 devices: a whole 2x2x4 slice. The times are simulated.
32 devices in a mesh: tile: 8 (over z, x), sec: 4 (over y, core).
Axes of the slice: x: 2, y: 2, z: 4, core: 2. Of those that a mesh axis runs over, the one named last changes fastest.
Arguments:
- displacement: float32 [8, 2, 128, 1024], P('sec', None, 'tile'), may hold values from -0.15 to 0.15
- velocity: float32 [8, 2, 128, 1024], P('sec', None, 'tile'), may hold values from -6 to 6
- stiffness: bfloat16 [8, 4, 128, 1024], P('sec', None, 'tile'), may hold values from 0.29882812 to 3
- anchor: float32 [2, 128, 1024], P(None, 'tile'), may hold values from -0.15 to 0.15
- match_source: int32 [8, 2048], P('sec', 'tile'), may hold values from 0 to 16383
- match_target: int32 [8, 2048], P('sec', 'tile'), may hold values from 0 to 16383
- match_weight: float32 [8, 2048], P('sec', 'tile'), may hold values from 1 to 8
- match_count: int32 [8, 8], P('sec', 'tile'), may hold values from 1 to 256, 1024 in all within a row
- reset_mask: int32 [2, 8], P(None, 'sec'), may hold values 0 or 1
Outputs:
- new_displacement: float32 [8, 2, 128, 1024], P('sec', None, 'tile')
- new_velocity: float32 [8, 2, 128, 1024], P('sec', None, 'tile')
Inputs may be any that keep to these rules, and one draw needn't show every extreme that they name: `match_count`: in every section the largest count is 256.
All inputs are finite; a program needn't handle non-finite values. No bound on the sum of `match_count` or of `reset_mask` on one device may be relied on, other than what follows from the above.
Results may differ from a plain program's by a relative error of at most 0.00055.
Values may be sent and summed in bfloat16 or wider, within the bound.
A program may use at most 128 MiB of HBM per device.

v0:
```python
import jax
import jax.numpy as jnp
from jax import lax
from jax.sharding import PartitionSpec as P

ITERS = 2


max_step = 0.05
time_step = 0.5
mixing = 0.1
epsilon = 1e-06
diagonal_rest = 1.4142135623730951


def from_behind(value, axis, steps):
    count = lax.axis_size(axis)
    leading, last = (max(0, -steps), min(count, count - steps))
    return lax.ppermute(value, axis, [(source, source + steps) for source in range(leading, last)])


def extended(block, sides, width):
    for axis, dim in sides:
        count = lax.axis_size(axis)
        forward = [(i, i + 1) for i in range(count - 1)]
        backward = [(target, source) for source, target in forward]
        low = lax.ppermute(
            lax.slice_in_dim(block, block.shape[dim] - width, None, axis=dim), axis, forward
        )
        high = lax.ppermute(lax.slice_in_dim(block, 0, width, axis=dim), axis, backward)
        block = jnp.concatenate([low, block, high], axis=dim)
    return block


def for_sending(value):

    def short(part):
        return part.astype(jnp.bfloat16) if part.dtype == jnp.float32 else part

    return jax.tree.map(short, value)


def from_left(values):
    return jnp.concatenate([jnp.zeros_like(values[..., :1]), values[..., :-1]], axis=-1)


def from_right(values):
    return jnp.concatenate([values[..., 1:], jnp.zeros_like(values[..., :1])], axis=-1)


def bond_force(first_gap, second_gap, spring_stiff, rest):
    stretch_len = jnp.sqrt(first_gap * first_gap + second_gap * second_gap)
    factor = spring_stiff * (stretch_len - rest) / stretch_len
    return (factor * first_gap, factor * second_gap)


def spring_force(padded, springs, row_start, total_rows):
    band_rows = padded.shape[-2] - 2
    columns = padded.shape[-1]
    stiff_all = springs.astype(jnp.float32)
    bond_rows = row_start - 1 + lax.iota(jnp.int32, band_rows + 1)
    row_valid = ((bond_rows >= 0) & (bond_rows + 1 < total_rows)).astype(jnp.float32)[:, None]
    column_ids = lax.iota(jnp.int32, columns)
    has_right = (column_ids < columns - 1).astype(jnp.float32)
    has_left = (column_ids >= 1).astype(jnp.float32)
    upper_first = padded[..., 0, :-1, :]
    upper_second = padded[..., 1, :-1, :]
    lower_first = padded[..., 0, 1:, :]
    lower_second = padded[..., 1, 1:, :]
    south = bond_force(
        1.0 + lower_first - upper_first,
        lower_second - upper_second,
        stiff_all[..., 1, :, :] * row_valid,
        1.0,
    )
    south_east = bond_force(
        1.0 + from_right(lower_first) - upper_first,
        1.0 + from_right(lower_second) - upper_second,
        stiff_all[..., 2, :, :] * row_valid * has_right,
        diagonal_rest,
    )
    south_west = bond_force(
        1.0 + from_left(lower_first) - upper_first,
        -1.0 + from_left(lower_second) - upper_second,
        stiff_all[..., 3, :, :] * row_valid * has_left,
        diagonal_rest,
    )
    middle_first = padded[..., 0, 1:-1, :]
    middle_second = padded[..., 1, 1:-1, :]
    east = bond_force(
        from_right(middle_first) - middle_first,
        1.0 + from_right(middle_second) - middle_second,
        stiff_all[..., 0, 1:, :] * has_right,
        1.0,
    )

    def summed(part):
        result = south[part][..., 1:, :] - south[part][..., :-1, :]
        result = result + south_east[part][..., 1:, :] - from_left(south_east[part][..., :-1, :])
        result = result + south_west[part][..., 1:, :] - from_right(south_west[part][..., :-1, :])
        return result + east[part] - from_left(east[part])

    return jnp.stack([summed(0), summed(1)], axis=-3)


def node_tables(index, band_rows, columns):
    row_table = (index[..., None] // columns == lax.iota(jnp.int32, band_rows)).astype(jnp.float32)
    column_table = (index[..., None] % columns == lax.iota(jnp.int32, columns)).astype(jnp.float32)
    return (row_table, column_table)


def pick_nodes(values, index, columns):
    sections = values.shape[0]
    band_rows = values.shape[2] // columns
    row_table, column_table = node_tables(index, band_rows, columns)
    grid = values.reshape(sections, 2, band_rows, columns)
    partial_rows = jnp.einsum("smc,skrc->skmr", column_table, grid, precision=lax.Precision.HIGHEST)
    return jnp.sum(partial_rows * row_table[:, None, :, :], axis=-1)


def place_nodes(target, index, amount, columns):
    sections = target.shape[0]
    band_rows = target.shape[2] // columns
    row_table, column_table = node_tables(index, band_rows, columns)
    spread = amount[..., None] * row_table[:, None, :, :]
    added = jnp.einsum("skmr,smc->skrc", spread, column_table, precision=lax.Precision.HIGHEST)
    return target + added.reshape(sections, 2, band_rows * columns)


def local(
    displacement,
    velocity,
    stiffness,
    anchor,
    match_source,
    match_target,
    match_weight,
    match_count,
    reset_mask,
):
    sections, _, band_rows, columns = displacement.shape
    slots = match_source.shape[1]
    nodes = band_rows * columns
    band_index = lax.axis_index("tile")
    band_total = lax.axis_size("tile")
    last_group = lax.axis_index("sec") == lax.axis_size("sec") - 1
    upper_stiff = from_behind(stiffness[:, 1:, band_rows - 1 :, :], "tile", 1)
    first_row = jnp.concatenate(
        [jnp.zeros((sections, 1, 1, columns), jnp.bfloat16), upper_stiff], axis=1
    )
    springs = jnp.concatenate([first_row, stiffness], axis=2)
    slot_live = (lax.iota(jnp.int32, slots)[None, :] < match_count).astype(jnp.float32)
    weight_live = match_weight * slot_live
    current = displacement
    speed = velocity
    for iteration in range(ITERS):
        padded = extended(current, (("tile", 2),), 1)
        force = spring_force(padded, springs, band_index * band_rows, band_total * band_rows)
        force = force.reshape(sections, 2, nodes)
        flat = current.reshape(sections, 2, nodes)
        source_points = pick_nodes(flat, match_source, columns)
        next_slab = from_behind(for_sending(current[0]), "sec", -1)
        next_slab = jnp.where(last_group, anchor, next_slab)
        following = jnp.concatenate([flat[1:], next_slab.reshape(1, 2, nodes)], axis=0)
        target_points = pick_nodes(following, match_target, columns)
        match_force = weight_live[:, None, :] * (target_points - source_points)
        force = place_nodes(force, match_source, match_force, columns)
        upper_part = place_nodes(force[1:], match_target[:-1], -match_force[:-1], columns)
        force = jnp.concatenate([force[:1], upper_part], axis=0)
        reaction = place_nodes(
            jnp.zeros((1, 2, nodes), jnp.float32), match_target[-1:], -match_force[-1:], columns
        )
        returned = from_behind(for_sending(reaction[0].reshape(2, band_rows, columns)), "sec", 1)
        force = jnp.concatenate([force[:1] + returned.reshape(1, 2, nodes), force[1:]], axis=0)
        force = force.reshape(sections, 2, band_rows, columns)
        velocity_mid = speed + time_step * force
        local_sums = (
            jnp.sum(force * force, axis=(1, 2, 3)),
            jnp.sum(velocity_mid * velocity_mid, axis=(1, 2, 3)),
        )
        force_sq, speed_sq = lax.psum((local_sums[0], local_sums[1]), "tile")
        speed_ratio = jnp.sqrt(speed_sq) / jnp.sqrt(force_sq + epsilon)
        speed = (1.0 - mixing) * velocity_mid + mixing * speed_ratio[:, None, None, None] * force
        keep = (1 - reset_mask[iteration]).astype(jnp.float32)
        speed = speed * keep[:, None, None, None]
        current = current + max_step * jnp.tanh(time_step * speed / max_step)
    return (current, speed)


def solution(mesh):
    placed = (
        P("sec", None, "tile", None),
        P("sec", None, "tile", None),
        P("sec", None, "tile", None),
        P(None, "tile", None),
        P("sec", "tile"),
        P("sec", "tile"),
        P("sec", "tile"),
        P("sec", "tile"),
        P(None, "sec"),
    )
    return jax.shard_map(
        local,
        mesh=mesh,
        in_specs=placed,
        out_specs=(P("sec", None, "tile", None), P("sec", None, "tile", None)),
        check_vma=False,
    )
```

profile of v0, /device:TPU:4, one launch (start us, length us, event | category | flops | bytes accessed | tf_op | source)
XLA Modules:
  0.0 88.7 jit_solution(14254812240650097541)
XLA Ops:
  0.7 1.1 %constant_dynamic-update-slice_fusion = (f32[2,2,17,1024]{3,2,0,1:T(8,128)S(1)}, f32[2,2,16,1024]{3,2,0,1:T(8,128)S(1)}) fusion(f32[2,2,16,1024]{3,2,1,0:T(8,128)} %param.9), kind=kLoop, calls=%fused_computation.195 | loop fusion | bytes 786432
  1.8 1.3 %collective-permute-start.1 = (f32[2,2,1,1024]{3,2,0,1:T(1,128)S(1)}, f32[2,2,1,1024]{3,2,0,1:T(1,128)S(1)}, u32[]{:S(2)}, u32[]{:S(2)}) collective-permute-start(f32[2,2,1,1024]{3,2,0,1:T(1,128)S(1)} %get-tuple-element.49), channel_id=1, source_target_pairs={{4,0},{8,4},{12,8},{16,12},{20,16},{24,20},{28,24},{5,1},{9,5},{13... | collective-permute-start | bytes 49160 | tf_op jit(solution)/shard_map/ppermute | solution.py:30
  3.2 4.5 %collective-permute-start = (bf16[2,3,1,1024]{3,2,0,1:T(2,128)(2,1)S(1)}, bf16[2,3,1,1024]{3,2,0,1:T(2,128)(2,1)S(1)}, u32[]{:S(2)}, u32[]{:S(2)}) collective-permute-start(bf16[2,3,1,1024]{3,2,0,1:T(2,128)(2,1)S(1)} %copy.36), channel_id=1, source_target_pairs={{0,4},{4,8},{8,12},{12,16},{16,20},{20,24},{24,28},{1,5},{5,9},{9,... | collective-permute-start | bytes 36872 | tf_op jit(solution)/shard_map/ppermute | solution.py:19
  7.7 4.3 %collective-permute-start.2 = (f32[2,2,1,1024]{3,2,0,1:T(1,128)S(1)}, f32[2,2,1,1024]{3,2,0,1:T(1,128)S(1)}, u32[]{:S(2)}, u32[]{:S(2)}) collective-permute-start(f32[2,2,1,1024]{3,2,0,1:T(1,128)S(1)} %get-tuple-element.48), channel_id=1, source_target_pairs={{0,4},{4,8},{8,12},{12,16},{16,20},{20,24},{24,28},{1,5},{5,9},{9,... | collective-permute-start | bytes 49160 | tf_op jit(solution)/shard_map/ppermute | solution.py:27
  12.1 1.9 %collective-permute-start.3 = (bf16[2,16,1024]{2,1,0:T(8,128)(2,1)S(1)}, bf16[2,16,1024]{2,1,0:T(8,128)(2,1)S(1)}, u32[]{:S(2)}, u32[]{:S(2)}) collective-permute-start(bf16[2,16,1024]{2,1,0:T(8,128)(2,1)S(1)} %fusion.118), channel_id=1, source_target_pairs={{1,0},{2,1},{3,2},{5,4},{6,5},{7,6},{9,8},{10,9},{11,10},{13,12},{... | collective-permute-start | bytes 196616 | tf_op jit(solution)/shard_map/ppermute | solution.py:19
  14.3 1.2 %fusion.44 = f32[2,256,2]{1,2,0:T(2,128)S(1)} fusion(f32[2,2,16,1024]{3,2,1,0:T(8,128)S(1)} %copy-done, s32[2,256]{1,0:T(2,128)S(1)} %get-tuple-element.69, f32[2,256,16]{1,2,0:T(8,128)S(1)} %fusion.131), kind=kOutput, calls=%fused_computation.22 | convolution fusion | flops 201882624 | bytes 301056 | tf_op jit(solution)/shard_map/smc,skrc->skmr/dot_general | solution.py:117
  18.5 1.2 %fusion.38 = f32[2,2,256]{2,1,0:T(2,128)S(1)} fusion(s32[2,256]{1,0:T(2,128)S(1)} %get-tuple-element.71, f32[1,2,16,1024]{3,2,1,0:T(8,128)S(1)} %select_bitcast_fusion.1, f32[1,2,16,1024]{3,2,1,0:T(8,128)S(1)} %slice-done, f32[2,256,16]{1,2,0:T(8,128)S(1)} %fusion.130), kind=kOutput, calls=%fused_computation.20 | convolution fusion | flops 201948160 | bytes 301056 | tf_op jit(solution)/shard_map/smc,skrc->skmr/dot_general | solution.py:117
  19.8 0.9 %fusion.10 = f32[2,2,16,1024]{3,2,1,0:T(8,128)S(1)} fusion(s32[2,256]{1,0:T(2,128)S(1)} %get-tuple-element.69, f32[2,256,16]{1,2,0:T(8,128)S(1)} %fusion.131, f32[2,2,256]{2,1,0:T(2,128)S(1)} %fusion.142), kind=kOutput, calls=%fused_computation.8 | convolution fusion | flops 201867264 | bytes 301056 | tf_op jit(solution)/shard_map/skmr,smc->skrc/dot_general | solution.py:126
  20.9 0.5 convolution_convert_fusion.1
  21.5 2.4 %collective-permute-start.4 = (bf16[2,16,1024]{2,1,0:T(8,128)(2,1)S(1)}, bf16[2,16,1024]{2,1,0:T(8,128)(2,1)S(1)}, u32[]{:S(2)}, u32[]{:S(2)}) collective-permute-start(bf16[2,16,1024]{2,1,0:T(8,128)(2,1)S(1)} %convolution_convert_fusion.1), channel_id=1, source_target_pairs={{0,1},{1,2},{2,3},{4,5},{5,6},{6,7},{8,9},{9,10},{10,11},{12,13},{... | collective-permute-start | bytes 196616 | tf_op jit(solution)/shard_map/ppermute | solution.py:19
  24.8 2.2 %collective-permute-done.4 = bf16[2,16,1024]{2,1,0:T(8,128)(2,1)S(1)} collective-permute-done((bf16[2,16,1024]{2,1,0:T(8,128)(2,1)S(1)}, bf16[2,16,1024]{2,1,0:T(8,128)(2,1)S(1)}, u32[]{:S(2)}, u32[]{:S(2)}) %collective-permute-start.4) | collective-permute-done | bytes 65568 | tf_op jit(solution)/shard_map/ppermute | solution.py:19
  28.3 18.0 %all-reduce.26 = (f32[2]{0:T(128)S(1)}, f32[2]{0:T(128)S(1)}) all-reduce(f32[2]{0:T(128)S(1)} %get-tuple-element.15, f32[2]{0:T(128)S(1)} %multiply_reduce_fusion.3), channel_id=1, replica_groups=mesh['tile'=8,'sec'=4] {'tile'}, use_global_device_ids=true, to_apply=%region_5.6 | all-reduce | flops 4 | bytes 32 | tf_op jit(solution)/shard_map/psum | solution.py:181
  46.6 1.3 %collective-permute-start.5 = (f32[2,2,1,1024]{3,2,0,1:T(1,128)S(1)}, f32[2,2,1,1024]{3,2,0,1:T(1,128)S(1)}, u32[]{:S(2)}, u32[]{:S(2)}) collective-permute-start(f32[2,2,1,1024]{3,2,0,1:T(1,128)S(1)} %get-tuple-element.43), channel_id=1, source_target_pairs={{4,0},{8,4},{12,8},{16,12},{20,16},{24,20},{28,24},{5,1},{9,5},{13... | collective-permute-start | bytes 49160 | tf_op jit(solution)/shard_map/ppermute | solution.py:30
  48.1 1.9 %collective-permute-start.7 = (bf16[2,16,1024]{2,1,0:T(8,128)(2,1)S(1)}, bf16[2,16,1024]{2,1,0:T(8,128)(2,1)S(1)}, u32[]{:S(2)}, u32[]{:S(2)}) collective-permute-start(bf16[2,16,1024]{2,1,0:T(8,128)(2,1)S(1)} %fusion.119), channel_id=1, source_target_pairs={{1,0},{2,1},{3,2},{5,4},{6,5},{7,6},{9,8},{10,9},{11,10},{13,12},{... | collective-permute-start | bytes 196616 | tf_op jit(solution)/shard_map/ppermute | solution.py:19
  50.1 1.2 %fusion.41 = f32[2,2,256]{2,1,0:T(2,128)S(1)} fusion(f32[2,2,16,1024]{3,2,1,0:T(8,128)S(1)} %get-tuple-element.13, s32[2,256]{1,0:T(2,128)S(1)} %get-tuple-element.69, f32[2,256,16]{1,2,0:T(8,128)S(1)} %fusion.131), kind=kOutput, calls=%fused_computation.21 | convolution fusion | flops 201882624 | bytes 301056 | tf_op jit(solution)/shard_map/smc,skrc->skmr/dot_general | solution.py:117
  51.3 4.5 %collective-permute-start.6 = (f32[2,2,1,1024]{3,2,0,1:T(1,128)S(1)}, f32[2,2,1,1024]{3,2,0,1:T(1,128)S(1)}, u32[]{:S(2)}, u32[]{:S(2)}) collective-permute-start(f32[2,2,1,1024]{3,2,0,1:T(1,128)S(1)} %get-tuple-element.42), channel_id=1, source_target_pairs={{0,4},{4,8},{8,12},{12,16},{16,20},{20,24},{24,28},{1,5},{5,9},{9,... | collective-permute-start | bytes 49160 | tf_op jit(solution)/shard_map/ppermute | solution.py:27
  56.5 0.8 collective-permute-done.6
  58.9 1.2 %fusion.35 = f32[2,2,256]{2,1,0:T(2,128)S(1)} fusion(s32[2,256]{1,0:T(2,128)S(1)} %get-tuple-element.71, f32[1,2,16,1024]{3,2,1,0:T(8,128)S(1)} %select_bitcast_fusion, f32[1,2,16,1024]{3,2,1,0:T(8,128)S(1)} %slice.408, f32[2,256,16]{1,2,0:T(8,128)S(1)} %fusion.130), kind=kOutput, calls=%fused_computation.19 | convolution fusion | flops 201948160 | bytes 301056 | tf_op jit(solution)/shard_map/smc,skrc->skmr/dot_general | solution.py:117
  60.1 0.9 %fusion.6 = f32[2,2,16,1024]{3,2,1,0:T(8,128)S(1)} fusion(s32[2,256]{1,0:T(2,128)S(1)} %get-tuple-element.69, f32[2,2,256]{2,1,0:T(2,128)S(1)} %subtract_multiply_fusion, f32[2,256,16]{1,2,0:T(8,128)S(1)} %fusion.131), kind=kOutput, calls=%fused_computation.6 | convolution fusion | flops 201867264 | bytes 301056 | tf_op jit(solution)/shard_map/skmr,smc->skrc/dot_general | solution.py:126
  61.8 1.9 %collective-permute-start.8 = (bf16[2,16,1024]{2,1,0:T(8,128)(2,1)S(1)}, bf16[2,16,1024]{2,1,0:T(8,128)(2,1)S(1)}, u32[]{:S(2)}, u32[]{:S(2)}) collective-permute-start(bf16[2,16,1024]{2,1,0:T(8,128)(2,1)S(1)} %convolution_convert_fusion), channel_id=1, source_target_pairs={{0,1},{1,2},{2,3},{4,5},{5,6},{6,7},{8,9},{9,10},{10,11},{12,13},{... | collective-permute-start | bytes 196616 | tf_op jit(solution)/shard_map/ppermute | solution.py:19
  64.0 0.5 fusion.57
  64.7 2.7 %collective-permute-done.8 = bf16[2,16,1024]{2,1,0:T(8,128)(2,1)S(1)} collective-permute-done((bf16[2,16,1024]{2,1,0:T(8,128)(2,1)S(1)}, bf16[2,16,1024]{2,1,0:T(8,128)(2,1)S(1)}, u32[]{:S(2)}, u32[]{:S(2)}) %collective-permute-start.8) | collective-permute-done | bytes 65568 | tf_op jit(solution)/shard_map/ppermute | solution.py:19
  68.3 19.4 %all-reduce.25 = (f32[2]{0:T(128)S(1)}, f32[2]{0:T(128)S(1)}) all-reduce(f32[2]{0:T(128)S(1)} %get-tuple-element.8, f32[2]{0:T(128)S(1)} %multiply_reduce_fusion.1), channel_id=1, replica_groups=mesh['tile'=8,'sec'=4] {'tile'}, use_global_device_ids=true, to_apply=%region_11.12 | all-reduce | flops 4 | bytes 32 | tf_op jit(solution)/shard_map/psum | solution.py:181
  87.7 0.9 %multiply_add_fusion = (f32[2,2,16,1024]{3,2,1,0:T(8,128)}, f32[2,2,16,1024]{3,2,1,0:T(8,128)}) fusion(f32[2,2,16,1024]{3,2,1,0:T(8,128)S(1)} %get-tuple-element.13, f32[2]{0:T(128)S(1)} %get-tuple-element.72, f32[2,2,16,1024]{3,2,1,0:T(8,128)S(1)} %reshape.483, f32[2]{0:T(128)S(1)} %multiply_multiply_fusion, f32[2,2,16,1024]{3,2,1,0:T(8,128)S(1)} %get-tuple-element.14), kind=kLoop, calls=%fused_computation.57 | loop fusion | flops 589824 | bytes 1310736 | tf_op jit(solution)/shard_map/add | solution.py:186
  (114 shorter events, 10.2 us)
Async XLA Ops:
  0.6 11.4 %copy-start = (f32[2,2,16,1024]{3,2,1,0:T(8,128)S(1)}, f32[2,2,16,1024]{3,2,1,0:T(8,128)}, u32[]{:S(2)}) copy-start(f32[2,2,16,1024]{3,2,1,0:T(8,128)} %param.9) | copy-start | bytes 786436
  0.6 2.4 %copy-start.3 = (bf16[2,4,16,1024]{3,2,1,0:T(8,128)(2,1)S(1)}, bf16[2,4,16,1024]{3,2,1,0:T(8,128)(2,1)}, u32[]{:S(2)}) copy-start(bf16[2,4,16,1024]{3,2,1,0:T(8,128)(2,1)} %param.11) | copy-start | bytes 786436
  0.7 13.4 %copy-start.4 = (s32[2,256]{1,0:T(2,128)S(1)}, s32[2,256]{1,0:T(2,128)}, u32[]{:S(2)}) copy-start(s32[2,256]{1,0:T(2,128)} %param.14) | copy-start | bytes 6148
  0.7 13.4 %copy-start.5 = (s32[2,256]{1,0:T(2,128)S(1)}, s32[2,256]{1,0:T(2,128)}, u32[]{:S(2)}) copy-start(s32[2,256]{1,0:T(2,128)} %param.13) | copy-start | bytes 6148
  0.7 13.6 %copy-start.7 = (s32[2,2]{1,0:T(2,128)S(1)}, s32[2,2]{1,0:T(2,128)}, u32[]{:S(2)}) copy-start(s32[2,2]{1,0:T(2,128)} %param.17) | copy-start | bytes 52
  1.8 14.2 %collective-permute-start.1 = (f32[2,2,1,1024]{3,2,0,1:T(1,128)S(1)}, f32[2,2,1,1024]{3,2,0,1:T(1,128)S(1)}, u32[]{:S(2)}, u32[]{:S(2)}) collective-permute-start(f32[2,2,1,1024]{3,2,0,1:T(1,128)S(1)} %get-tuple-element.49), channel_id=1, source_target_pairs={{4,0},{8,4},{12,8},{16,12},{20,16},{24,20},{28,24},{5,1},{9,5},{13... | collective-permute-start | bytes 49160 | tf_op jit(solution)/shard_map/ppermute | solution.py:30
  3.2 12.6 %collective-permute-start = (bf16[2,3,1,1024]{3,2,0,1:T(2,128)(2,1)S(1)}, bf16[2,3,1,1024]{3,2,0,1:T(2,128)(2,1)S(1)}, u32[]{:S(2)}, u32[]{:S(2)}) collective-permute-start(bf16[2,3,1,1024]{3,2,0,1:T(2,128)(2,1)S(1)} %copy.36), channel_id=1, source_target_pairs={{0,4},{4,8},{8,12},{12,16},{16,20},{20,24},{24,28},{1,5},{5,9},{9,... | collective-permute-start | bytes 36872 | tf_op jit(solution)/shard_map/ppermute | solution.py:19
  7.7 8.8 %collective-permute-start.2 = (f32[2,2,1,1024]{3,2,0,1:T(1,128)S(1)}, f32[2,2,1,1024]{3,2,0,1:T(1,128)S(1)}, u32[]{:S(2)}, u32[]{:S(2)}) collective-permute-start(f32[2,2,1,1024]{3,2,0,1:T(1,128)S(1)} %get-tuple-element.48), channel_id=1, source_target_pairs={{0,4},{4,8},{8,12},{12,16},{16,20},{20,24},{24,28},{1,5},{5,9},{9,... | collective-permute-start | bytes 49160 | tf_op jit(solution)/shard_map/ppermute | solution.py:27
  12.1 5.9 %collective-permute-start.3 = (bf16[2,16,1024]{2,1,0:T(8,128)(2,1)S(1)}, bf16[2,16,1024]{2,1,0:T(8,128)(2,1)S(1)}, u32[]{:S(2)}, u32[]{:S(2)}) collective-permute-start(bf16[2,16,1024]{2,1,0:T(8,128)(2,1)S(1)} %fusion.118), channel_id=1, source_target_pairs={{1,0},{2,1},{3,2},{5,4},{6,5},{7,6},{9,8},{10,9},{11,10},{13,12},{... | collective-permute-start | bytes 196616 | tf_op jit(solution)/shard_map/ppermute | solution.py:19
  14.0 1.5 %copy-start.6 = (f32[2,256]{1,0:T(2,128)S(1)}, f32[2,256]{1,0:T(2,128)}, u32[]{:S(2)}) copy-start(f32[2,256]{1,0:T(2,128)} %param.15) | copy-start | bytes 6148
  14.0 1.5 %copy-start.8 = (s32[2,1]{0,1:T(1,128)S(1)}, s32[2,1]{0,1:T(1,128)}, u32[]{:S(2)}) copy-start(s32[2,1]{0,1:T(1,128)} %param.16) | copy-start | bytes 28
  17.4 0.9 %copy-start.2 = (f32[2,16,1024]{2,1,0:T(8,128)S(1)}, f32[2,16,1024]{2,1,0:T(8,128)}, u32[]{:S(2)}) copy-start(f32[2,16,1024]{2,1,0:T(8,128)} %param.12) | copy-start | bytes 393220
  17.6 0.9 %slice-start = ((f32[2,2,16,1024]{3,2,1,0:T(8,128)}), f32[1,2,16,1024]{3,2,1,0:T(8,128)S(1)}, s32[]{:S(2)}) async-start(f32[2,2,16,1024]{3,2,1,0:T(8,128)} %param.9), calls=%async_computation | async-start | bytes 262144 | tf_op jit(solution)/shard_map/slice | solution.py:164
  21.5 5.6 %collective-permute-start.4 = (bf16[2,16,1024]{2,1,0:T(8,128)(2,1)S(1)}, bf16[2,16,1024]{2,1,0:T(8,128)(2,1)S(1)}, u32[]{:S(2)}, u32[]{:S(2)}) collective-permute-start(bf16[2,16,1024]{2,1,0:T(8,128)(2,1)S(1)} %convolution_convert_fusion.1), channel_id=1, source_target_pairs={{0,1},{1,2},{2,3},{4,5},{5,6},{6,7},{8,9},{9,10},{10,11},{12,13},{... | collective-permute-start | bytes 196616 | tf_op jit(solution)/shard_map/ppermute | solution.py:19
  27.2 1.0 %copy-start.1 = (f32[2,2,16,1024]{3,2,1,0:T(8,128)S(1)}, f32[2,2,16,1024]{3,2,1,0:T(8,128)}, u32[]{:S(2)}) copy-start(f32[2,2,16,1024]{3,2,1,0:T(8,128)} %param.10) | copy-start | bytes 786436
  46.6 9.3 %collective-permute-start.5 = (f32[2,2,1,1024]{3,2,0,1:T(1,128)S(1)}, f32[2,2,1,1024]{3,2,0,1:T(1,128)S(1)}, u32[]{:S(2)}, u32[]{:S(2)}) collective-permute-start(f32[2,2,1,1024]{3,2,0,1:T(1,128)S(1)} %get-tuple-element.43), channel_id=1, source_target_pairs={{4,0},{8,4},{12,8},{16,12},{20,16},{24,20},{28,24},{5,1},{9,5},{13... | collective-permute-start | bytes 49160 | tf_op jit(solution)/shard_map/ppermute | solution.py:30
  48.1 10.8 %collective-permute-start.7 = (bf16[2,16,1024]{2,1,0:T(8,128)(2,1)S(1)}, bf16[2,16,1024]{2,1,0:T(8,128)(2,1)S(1)}, u32[]{:S(2)}, u32[]{:S(2)}) collective-permute-start(bf16[2,16,1024]{2,1,0:T(8,128)(2,1)S(1)} %fusion.119), channel_id=1, source_target_pairs={{1,0},{2,1},{3,2},{5,4},{6,5},{7,6},{9,8},{10,9},{11,10},{13,12},{... | collective-permute-start | bytes 196616 | tf_op jit(solution)/shard_map/ppermute | solution.py:19
  51.3 6.0 %collective-permute-start.6 = (f32[2,2,1,1024]{3,2,0,1:T(1,128)S(1)}, f32[2,2,1,1024]{3,2,0,1:T(1,128)S(1)}, u32[]{:S(2)}, u32[]{:S(2)}) collective-permute-start(f32[2,2,1,1024]{3,2,0,1:T(1,128)S(1)} %get-tuple-element.42), channel_id=1, source_target_pairs={{0,4},{4,8},{8,12},{12,16},{16,20},{20,24},{24,28},{1,5},{5,9},{9,... | collective-permute-start | bytes 49160 | tf_op jit(solution)/shard_map/ppermute | solution.py:27
  61.8 5.6 %collective-permute-start.8 = (bf16[2,16,1024]{2,1,0:T(8,128)(2,1)S(1)}, bf16[2,16,1024]{2,1,0:T(8,128)(2,1)S(1)}, u32[]{:S(2)}, u32[]{:S(2)}) collective-permute-start(bf16[2,16,1024]{2,1,0:T(8,128)(2,1)S(1)} %convolution_convert_fusion), channel_id=1, source_target_pairs={{0,1},{1,2},{2,3},{4,5},{5,6},{6,7},{8,9},{9,10},{10,11},{12,13},{... | collective-permute-start | bytes 196616 | tf_op jit(solution)/shard_map/ppermute | solution.py:19
where the time goes:
time: 89.1 us; the launch traced here: 88.7 us
  blocking collectives  37.4 us (42%)
  starting transfers between devices  24.1 us (27%)
  matrix products  8.77 us (10%)
  local copies, waits for them, and re-layouts  5.92 us (7%)
  waiting for transfers between devices  5.73 us (6%)
  other arithmetic  5.21 us (6%)
  between operations  1.51 us (2%)
    psum x2, blocking collectives, local(): force_sq, speed_sq = lax.psum((local_sums[0], local_sums[1]), 'tile')  37.4 us
    ppermute x5, starting transfers between devices, from_behind(): lax.ppermute(value, axis, [(source, source + steps) for source in range(l...  12.7 us
    ppermute x2, starting transfers between devices, extended(): lax.ppermute(lax.slice_in_dim(block, block.shape[dim] - width, None, axis...  8.84 us
    ppermute x5, waiting for transfers between devices, from_behind(): lax.ppermute(value, axis, [(source, source + steps) for source in range(l...  4.92 us
    dot_general x4, matrix products, pick_nodes(): jnp.einsum('smc,skrc->skmr', column_table, grid, precision=lax.Precision....  4.82 us
    dot_general x6, matrix products, place_nodes(): jnp.einsum('skmr,smc->skrc', spread, column_table, precision=lax.Precisio...  3.95 us
    ppermute x2, starting transfers between devices, extended(): lax.ppermute(lax.slice_in_dim(block, 0, width, axis=dim), axis, backward)  2.58 us
  transfers between devices with their start and end apart: 9, of which 3 were waited for; matrix products, arithmetic and copies ran while one was open for 10% of the time, Pallas kernels for 0%

commit v1 on v0

v1 whole, which is shorter than its diff:
```python
import functools

import jax
import jax.numpy as jnp
from jax import lax
from jax.experimental import pallas as pl
from jax.experimental.pallas import tpu as pltpu
from jax.sharding import PartitionSpec as P

ITERS = 2

max_step = 0.05
time_step = 0.5
mixing = 0.1
epsilon = 1e-06
diagonal_rest = 1.4142135623730951
MESH = pl.DeviceIdType.MESH
F32 = jnp.float32
BF16 = jnp.bfloat16


def split(value):
    high = value.astype(BF16)
    return high, (value - high.astype(F32)).astype(BF16)


def from_left(values):
    return pltpu.roll(values, 1, 1)


def from_right(values):
    return pltpu.roll(values, values.shape[1] - 1, 1)


def bond(first_gap, second_gap, stiff, rest):
    inverse = lax.rsqrt(first_gap * first_gap + second_gap * second_gap)
    factor = stiff * (1.0 - rest * inverse)
    return factor * first_gap, factor * second_gap


def downward(upper, lower, lower_right, lower_left, stiff):
    south = bond(1.0 + lower[0] - upper[0], lower[1] - upper[1], stiff[0], 1.0)
    east = bond(
        1.0 + lower_right[0] - upper[0], 1.0 + lower_right[1] - upper[1], stiff[1], diagonal_rest
    )
    west = bond(
        1.0 + lower_left[0] - upper[0], lower_left[1] - upper[1] - 1.0, stiff[2], diagonal_rest
    )
    owned = tuple(south[i] + east[i] + west[i] for i in range(2))
    ended = tuple(south[i] + from_left(east[i]) + from_right(west[i]) for i in range(2))
    return owned, ended


def stacked(grid, rows):
    columns = grid.shape[1]
    return jnp.concatenate([grid[:, i : i + 128] for i in range(0, columns, 128)], axis=0)


def unstacked(values, rows):
    return jnp.concatenate([values[i : i + rows] for i in range(0, values.shape[0], rows)], axis=1)


def tables(index, rows, columns):
    pieces = columns // 128
    slots = index.shape[1]
    low = lax.rem(index, 128)
    row = index // columns
    place = (lax.rem(index, columns) // 128) * rows + row
    column_table = (lax.broadcasted_iota(jnp.int32, (128, slots), 0) == low).astype(F32).astype(BF16)
    row_table = (lax.broadcasted_iota(jnp.int32, (pieces * rows, slots), 0) == place).astype(F32)
    return column_table, row_table


def pick(parts, column_table, row_table):
    result = []
    for high, low in parts:
        found = jnp.dot(high, column_table, preferred_element_type=F32)
        found = found + jnp.dot(low, column_table, preferred_element_type=F32)
        result.append(jnp.sum(found * row_table, axis=0, keepdims=True))
    return result


def place(amount, column_table, row_table, rows):
    spread = amount * row_table
    high, low = split(spread)
    dims = (((1,), (1,)), ((), ()))
    out = lax.dot_general(high, column_table, dims, preferred_element_type=F32)
    out = out + lax.dot_general(low, column_table, dims, preferred_element_type=F32)
    return unstacked(out, rows)


def kernel(
    n_tile,
    n_sec,
    u_hbm,
    v_hbm,
    k_hbm,
    a_hbm,
    src_hbm,
    tgt_hbm,
    w_hbm,
    cnt,
    rst,
    out_u,
    out_v,
    u_ref,
    v_ref,
    k_ref,
    a_ref,
    src_ref,
    tgt_ref,
    w_ref,
    kf_ref,
    force_ref,
    mid_ref,
    ctab_ref,
    rtab_ref,
    in_sem,
    out_sem,
    down_send,
    up_send,
    down_recv,
    up_recv,
    edge_send,
    edge_recv,
    slot_send,
    slot_recv,
    points_send,
    points_recv,
    sums_send,
    sums_recv,
    near_ssem,
    near_rsem,
    sums_ssem,
    sums_rsem,
):
    tile = lax.axis_index("tile")
    sec = lax.axis_index("sec")
    sections, _, rows, columns = u_ref.shape
    slots = src_ref.shape[1]
    below, above = lax.rem(tile + 1, n_tile), lax.rem(tile + n_tile - 1, n_tile)
    after, before = lax.rem(sec + 1, n_sec), lax.rem(sec + n_sec - 1, n_sec)

    loads = [
        pltpu.make_async_copy(source, target, in_sem.at[i])
        for i, (source, target) in enumerate(
            [
                (u_hbm, u_ref),
                (k_hbm, k_ref),
                (src_hbm, src_ref),
                (tgt_hbm, tgt_ref),
                (w_hbm, w_ref),
                (a_hbm, a_ref),
                (v_hbm, v_ref),
            ]
        )
    ]
    for load in loads:
        load.start()

    barrier = pltpu.get_barrier_semaphore()
    for step in range(1, n_tile):
        pl.semaphore_signal(
            barrier, inc=1, device_id=(lax.rem(tile + step, n_tile), sec), device_id_type=MESH
        )
    for other in (after, before):
        pl.semaphore_signal(barrier, inc=1, device_id=(tile, other), device_id_type=MESH)

    def remote(source, target, ssem, rsem, device):
        copy = pltpu.make_async_remote_copy(
            src_ref=source,
            dst_ref=target,
            send_sem=ssem,
            recv_sem=rsem,
            device_id=device,
            device_id_type=MESH,
        )
        copy.start()
        return copy

    def near(number, source, target, device):
        return remote(source, target, near_ssem.at[number], near_rsem.at[number], device)

    for load in loads[:5]:
        load.wait()

    column_ids = lax.broadcasted_iota(jnp.int32, (1, columns), 1)
    has_right = (column_ids < columns - 1).astype(F32)
    has_left = (column_ids >= 1).astype(F32)
    for s in range(sections):
        for i in range(2):
            down_send[2 * s + i : 2 * s + i + 1, :] = u_ref[s, i, rows - 1 : rows, :]
            up_send[2 * s + i : 2 * s + i + 1, :] = u_ref[s, i, 0:1, :]
        for kind in range(4):
            stiff = k_ref[s, kind].astype(F32)
            if kind in (0, 2):
                stiff = stiff * has_right
            if kind == 3:
                stiff = stiff * has_left
            kf_ref[s, kind] = stiff
            if kind > 0:
                at = 8 + 2 * (kind - 1) + s
                down_send[at : at + 1, :] = stiff[rows - 1 : rows, :]

    slot_ids = lax.broadcasted_iota(jnp.int32, (1, slots), 1)
    weights = [
        w_ref[s : s + 1, :] * (slot_ids < cnt[s, 0]).astype(F32) for s in range(sections)
    ]

    def store_tables(number, index):
        column_table, row_table = tables(index, rows, columns)
        ctab_ref[number] = column_table
        rtab_ref[number] = row_table

    def picked(number, parts):
        return pick(parts, ctab_ref[number], rtab_ref[number])

    def placed(number, amount):
        return place(amount, ctab_ref[number], rtab_ref[number], rows)

    def parts_of(ref, s=None):
        return [
            split(stacked(ref[i] if s is None else ref[s, i], rows)) for i in range(2)
        ]

    store_tables(1, src_ref[1:2, :])
    parts_1 = parts_of(u_ref, 1)
    points_1 = picked(1, parts_1)
    slot_send[0, 0:1, :] = tgt_ref[1:2, :].astype(F32)
    slot_send[0, 1:2, :] = weights[1]
    slot_send[0, 2:3, :] = points_1[0]
    slot_send[0, 3:4, :] = points_1[1]

    pl.semaphore_wait(barrier, n_tile + 1)
    copies = [
        near(0, slot_send.at[0], slot_recv.at[0], (tile, after)),
        near(1, down_send, down_recv, (below, sec)),
        near(2, up_send, up_recv, (above, sec)),
    ]
    slots_in, down_in, up_in = copies

    store_tables(0, src_ref[0:1, :])
    store_tables(2, tgt_ref[0:1, :])
    parts_0 = parts_of(u_ref, 0)
    points_0 = picked(0, parts_0)
    ends_0 = picked(2, parts_1)
    loads[5].wait()
    first_sec = sec == 0

    def slab_parts():
        return [
            split(stacked(jnp.where(first_sec, a_ref[i], u_ref[0, i]), rows)) for i in range(2)
        ]

    slots_in.wait_recv()
    store_tables(3, slot_recv[0, 0:1, :].astype(jnp.int32))
    weight_in = slot_recv[0, 1:2, :] * jnp.where(first_sec, 0.0, 1.0)
    ends_in = picked(3, slab_parts())
    points_in = [slot_recv[0, 2:3, :], slot_recv[0, 3:4, :]]
    points_send[0, 0:1, :] = ends_in[0]
    points_send[0, 1:2, :] = ends_in[1]
    points = near(3, points_send.at[0], points_recv.at[0], (tile, before))
    copies.append(points)

    loads[6].wait()
    not_last = jnp.where(tile == n_tile - 1, 0.0, 1.0)
    not_first = jnp.where(tile == 0, 0.0, 1.0)
    row_ids = lax.broadcasted_iota(jnp.int32, (rows, columns), 0)
    row_valid = jnp.where(row_ids == rows - 1, not_last, 1.0)
    for s in range(sections):
        for kind in range(1, 4):
            kf_ref[s, kind] = kf_ref[s, kind] * row_valid

    down_in.wait_recv()
    up_in.wait_recv()
    halo_up = down_recv[0:4, :]
    halo_down = up_recv[0:4, :]
    stiff_up = [down_recv[8 + 2 * i : 10 + 2 * i, :] * not_first for i in range(3)]
    speed_ratio = None

    for iteration in range(ITERS):
        upper = [
            jnp.concatenate([halo_up[i : i + 1], halo_up[2 + i : 3 + i]], axis=0)
            for i in range(2)
        ]
        lower = [
            jnp.concatenate([u_ref[0, i, 0:1, :], u_ref[1, i, 0:1, :]], axis=0)
            for i in range(2)
        ]
        _, ended_up = downward(
            upper,
            lower,
            [from_right(x) for x in lower],
            [from_left(x) for x in lower],
            stiff_up,
        )
        for s in range(sections):
            own = [u_ref[s, i] for i in range(2)]
            right = [from_right(x) for x in own]
            left = [from_left(x) for x in own]
            tail = [halo_down[2 * s + i : 2 * s + i + 1] for i in range(2)]
            lower = [jnp.concatenate([own[i][1:], tail[i]], axis=0) for i in range(2)]
            lower_right = [
                jnp.concatenate([right[i][1:], from_right(tail[i])], axis=0) for i in range(2)
            ]
            lower_left = [
                jnp.concatenate([left[i][1:], from_left(tail[i])], axis=0) for i in range(2)
            ]
            owned, ended = downward(
                own, lower, lower_right, lower_left, [kf_ref[s, kind] for kind in (1, 2, 3)]
            )
            east = bond(right[0] - own[0], 1.0 + right[1] - own[1], kf_ref[s, 0], 1.0)
            for i in range(2):
                incoming = jnp.concatenate(
                    [ended_up[i][s : s + 1], ended[i][: rows - 1]], axis=0
                )
                force_ref[s, i] = owned[i] + east[i] - from_left(east[i]) - incoming

        match_0 = [weights[0] * (ends_0[i] - points_0[i]) for i in range(2)]
        match_in = [weight_in * (ends_in[i] - points_in[i]) for i in range(2)]
        points.wait_recv()
        sums = []
        for i in range(2):
            found = points_recv[iteration, i : i + 1, :]
            match_1 = weights[1] * (found - points_1[i])
            force_ref[0, i] = force_ref[0, i] + placed(0, match_0[i]) - placed(3, match_in[i])
            force_ref[1, i] = force_ref[1, i] + placed(1, match_1) - placed(2, match_0[i])

        for s in range(sections):
            force_sq, speed_sq = 0.0, 0.0
            for i in range(2):
                force = force_ref[s, i]
                middle = v_ref[s, i] + time_step * force
                mid_ref[s, i] = middle
                force_sq = force_sq + jnp.sum(force * force, axis=0, keepdims=True)
                speed_sq = speed_sq + jnp.sum(middle * middle, axis=0, keepdims=True)
                if iteration < ITERS - 1:
                    at = 2 * s + i
                    edge_send[0, at : at + 1, :] = force[rows - 1 : rows, :]
                    edge_send[0, 4 + at : 5 + at, :] = middle[rows - 1 : rows, :]
                    edge_send[1, at : at + 1, :] = force[0:1, :]
                    edge_send[1, 4 + at : 5 + at, :] = middle[0:1, :]
            for at, value in ((s, force_sq), (2 + s, speed_sq)):
                narrow = value[:, 0:128]
                for piece in range(128, columns, 128):
                    narrow = narrow + value[:, piece : piece + 128]
                sums_send[iteration, at : at + 1, :] = narrow
        peers = []
        for step in range(n_tile - 1, 0, -1):
            peers.append(
                remote(
                    sums_send.at[iteration],
                    sums_recv.at[iteration, step - 1],
                    sums_ssem.at[iteration, step - 1],
                    sums_rsem.at[iteration, step - 1],
                    (lax.rem(tile + step, n_tile), sec),
                )
            )
        copies += peers
        if iteration < ITERS - 1:
            edge_down = near(4, edge_send.at[0], edge_recv.at[0], (below, sec))
            edge_up = near(5, edge_send.at[1], edge_recv.at[1], (above, sec))
            copies += [edge_down, edge_up]

        total = sums_send[iteration, 0:4, :]
        for peer in peers:
            peer.wait_recv()
        for step in range(n_tile - 1):
            total = total + sums_recv[iteration, step, 0:4, :]
        total = jnp.sum(total, axis=1, keepdims=True)
        ratio = jnp.sqrt(total[2:4]) / jnp.sqrt(total[0:2] + epsilon)
        keep = [(1 - rst[iteration, s]).astype(F32) for s in range(sections)]

        for s in range(sections):
            push = mixing * ratio[s : s + 1, :]
            for i in range(2):
                speed = ((1.0 - mixing) * mid_ref[s, i] + push * force_ref[s, i]) * keep[s]
                v_ref[s, i] = speed
                u_ref[s, i] = u_ref[s, i] + max_step * jnp.tanh(time_step / max_step * speed)

        if iteration < ITERS - 1:
            parts_1 = parts_of(u_ref, 1)
            points_1 = picked(1, parts_1)
            slot_send[1, 0:1, :] = points_1[0]
            slot_send[1, 1:2, :] = points_1[1]
            slots_in = near(6, slot_send.at[1], slot_recv.at[1], (tile, after))
            ends_in = picked(3, slab_parts())
            points_send[1, 0:1, :] = ends_in[0]
            points_send[1, 1:2, :] = ends_in[1]
            points = near(7, points_send.at[1], points_recv.at[1], (tile, before))
            copies += [slots_in, points]
            points_0 = picked(0, parts_of(u_ref, 0))
            ends_0 = picked(2, parts_1)

            half = lax.broadcasted_iota(jnp.int32, (4, columns), 0) < 2
            ratio_rows = jnp.where(half, mixing * ratio[0:1, :], mixing * ratio[1:2, :])
            keep_rows = jnp.where(half, keep[0], keep[1])

            def moved(halo, edge):
                speed = ((1.0 - mixing) * edge[4:8, :] + ratio_rows * edge[0:4, :]) * keep_rows
                return halo + max_step * jnp.tanh(time_step / max_step * speed)

            edge_down.wait_recv()
            edge_up.wait_recv()
            halo_up = moved(halo_up, edge_recv[0])
            halo_down = moved(halo_down, edge_recv[1])
            slots_in.wait_recv()
            points_in = [slot_recv[1, 0:1, :], slot_recv[1, 1:2, :]]

    stores = [
        pltpu.make_async_copy(v_ref, out_v, out_sem.at[0]),
        pltpu.make_async_copy(u_ref, out_u, out_sem.at[1]),
    ]
    for store in stores:
        store.start()
    for copy in copies:
        copy.wait_send()
    for store in stores:
        store.wait()


def local(n_tile, n_sec, *arguments):
    displacement, velocity, stiffness, anchor, source, target, weight, _, _ = arguments
    sections, _, rows, columns = displacement.shape
    slots = source.shape[1]
    pieces = columns // 128
    dma = pltpu.SemaphoreType.DMA
    anywhere = pl.BlockSpec(memory_space=pl.ANY)
    scalars = pl.BlockSpec(memory_space=pltpu.SMEM)
    field = jax.ShapeDtypeStruct(displacement.shape, F32)
    vmem = pltpu.VMEM
    return pl.pallas_call(
        functools.partial(kernel, n_tile, n_sec),
        out_shape=(field, field),
        in_specs=[anywhere] * 7 + [scalars] * 2,
        out_specs=(anywhere, anywhere),
        scratch_shapes=[
            vmem(displacement.shape, F32),
            vmem(velocity.shape, F32),
            vmem(stiffness.shape, BF16),
            vmem(anchor.shape, F32),
            vmem(source.shape, jnp.int32),
            vmem(target.shape, jnp.int32),
            vmem(weight.shape, F32),
            vmem(stiffness.shape, F32),
            vmem(displacement.shape, F32),
            vmem(displacement.shape, F32),
            vmem((4, 128, slots), BF16),
            vmem((4, pieces * rows, slots), F32),
            dma((7,)),
            dma((2,)),
            vmem((16, columns), F32),
            vmem((8, columns), F32),
            vmem((16, columns), F32),
            vmem((8, columns), F32),
            vmem((2, 8, columns), F32),
            vmem((2, 8, columns), F32),
            vmem((2, 8, slots), F32),
            vmem((2, 8, slots), F32),
            vmem((2, 8, slots), F32),
            vmem((2, 8, slots), F32),
            vmem((ITERS, 8, 128), F32),
            vmem((ITERS, n_tile - 1, 8, 128), F32),
            dma((8,)),
            dma((8,)),
            dma((ITERS, n_tile - 1)),
            dma((ITERS, n_tile - 1)),
        ],
        compiler_params=pltpu.CompilerParams(
            collective_id=0, has_side_effects=True, vmem_limit_bytes=60 * 1024 * 1024
        ),
        cost_estimate=pl.CostEstimate(
            flops=40_000_000, bytes_accessed=1_500_000, transcendentals=1_000_000
        ),
    )(*arguments)


def solution(mesh):
    placed = (
        P("sec", None, "tile", None),
        P("sec", None, "tile", None),
        P("sec", None, "tile", None),
        P(None, "tile", None),
        P("sec", "tile"),
        P("sec", "tile"),
        P("sec", "tile"),
        P("sec", "tile"),
        P(None, "sec"),
    )
    return jax.shard_map(
        functools.partial(local, mesh.shape["tile"], mesh.shape["sec"]),
        mesh=mesh,
        in_specs=placed,
        out_specs=(P("sec", None, "tile", None), P("sec", None, "tile", None)),
        check_vma=False,
    )
```

time: 89.1 us -> 28.7 us (0.32)
  the two profiles are of different devices: /device:TPU:4 before, /device:TPU:0 now
where the time goes in v1:
time: 28.7 us; the launch traced here: 28.5 us
  Pallas kernels  24.1 us (84%)
  local copies, waits for them, and re-layouts  3.72 us (13%)
  between operations  0.65 us (2%)
    pallas_call x1, Pallas kernels, local(): pl.pallas_call(functools.partial(kernel, n_tile, n_sec), out_shape=(field...  24.1 us
    unnamed x5, local copies, waits for them, and re-layouts  3.72 us

profile of v1, /device:TPU:0, one launch (start us, length us, event | category | flops | bytes accessed | tf_op | source)
XLA Modules:
  0.0 28.5 jit_solution(6038722863794769980)
XLA Ops:
  0.6 1.3 %copy.11.cnt = s32[2,1]{1,0:T(2,128)} copy(s32[2,1]{0,1:T(1,128)} %param.16) | data formatting | bytes 16 | tf_op args[7]
  1.9 24.1 %shard_map.104 = (f32[2,2,16,1024]{3,2,1,0:T(8,128)}, f32[2,2,16,1024]{3,2,1,0:T(8,128)}) custom-call(f32[2,2,16,1024]{3,2,1,0:T(8,128)} %u_hbm.1, f32[2,2,16,1024]{3,2,1,0:T(8,128)} %v_hbm.1, bf16[2,4,16,1024]{3,2,1,0:T(8,128)(2,1)} %k_hbm.1, f32[2,16,1024]{2,1,0:T(8,128)} %a_hbm.1, s32[2,256]{1,0:T(2,128)} %src_hbm.1, s32[2,256]{1,0:T(2,128)} %tgt_hbm.1, ...), custom_call_target="tpu_custom_call" | custom-call | flops 40000000 | bytes 1500000 | tf_op jit(solution)/shard_map/pallas_call | solution.py:432
  26.1 0.0 copy-start
  26.1 1.7 %copy.14 = f32[2,2,16,1024]{3,2,1,0:T(8,128)} copy(f32[2,2,16,1024]{3,2,1,0:T(8,128)} %get-tuple-element.4) | data formatting | bytes 524288
  27.8 0.0 copy-done
  27.8 0.7 %copy.15 = f32[2,2,16,1024]{3,2,1,0:T(8,128)} copy(f32[2,2,16,1024]{3,2,1,0:T(8,128)S(1)} %copy-done) | data formatting | bytes 524288
Async XLA Ops:
  26.1 1.7 %copy-start = (f32[2,2,16,1024]{3,2,1,0:T(8,128)S(1)}, f32[2,2,16,1024]{3,2,1,0:T(8,128)}, u32[]{:S(2)}) copy-start(f32[2,2,16,1024]{3,2,1,0:T(8,128)} %get-tuple-element.5) | copy-start | bytes 786436

commit v2 on v1

--- a/solution.py
+++ b/solution.py
@@ -72,21 +72,27 @@
 
 
 def pick(parts, column_table, row_table):
+    found = jnp.dot(parts, column_table, preferred_element_type=F32)
+    nodes = row_table.shape[0]
     result = []
-    for high, low in parts:
-        found = jnp.dot(high, column_table, preferred_element_type=F32)
-        found = found + jnp.dot(low, column_table, preferred_element_type=F32)
-        result.append(jnp.sum(found * row_table, axis=0, keepdims=True))
+    for i in range(2):
+        both = found[i * nodes : (i + 1) * nodes] + found[(2 + i) * nodes : (3 + i) * nodes]
+        result.append(jnp.sum(both * row_table, axis=0, keepdims=True))
     return result
 
 
-def place(amount, column_table, row_table, rows):
-    spread = amount * row_table
-    high, low = split(spread)
-    dims = (((1,), (1,)), ((), ()))
-    out = lax.dot_general(high, column_table, dims, preferred_element_type=F32)
-    out = out + lax.dot_general(low, column_table, dims, preferred_element_type=F32)
-    return unstacked(out, rows)
+def place(amounts, column_table, row_table, rows):
+    highs = [amount.astype(BF16).astype(F32) for amount in amounts]
+    lows = [amount - high for amount, high in zip(amounts, highs)]
+    spread = jnp.concatenate([(x * row_table).astype(BF16) for x in highs + lows], axis=0)
+    out = lax.dot_general(
+        spread, column_table, (((1,), (1,)), ((), ())), preferred_element_type=F32
+    )
+    nodes = row_table.shape[0]
+    return [
+        unstacked(out[i * nodes : (i + 1) * nodes] + out[(2 + i) * nodes : (3 + i) * nodes], rows)
+        for i in range(2)
+    ]
 
 
 def kernel(
@@ -101,8 +107,11 @@
     w_hbm,
     cnt,
     rst,
+    out_mid,
+    out_force,
     out_u,
-    out_v,
+    out_push,
+    out_decay,
     u_ref,
     v_ref,
     k_ref,
@@ -115,6 +124,8 @@
     mid_ref,
     ctab_ref,
     rtab_ref,
+    push_ref,
+    decay_ref,
     in_sem,
     out_sem,
     down_send,
@@ -204,28 +215,32 @@
 
     slot_ids = lax.broadcasted_iota(jnp.int32, (1, slots), 1)
     weights = [
-        w_ref[s : s + 1, :] * (slot_ids < cnt[s, 0]).astype(F32) for s in range(sections)
+        w_ref[s : s + 1, :] * (slot_ids < cnt[0, s]).astype(F32) for s in range(sections)
     ]
 
-    def store_tables(number, index):
+    def store_tables(section, half, index):
         column_table, row_table = tables(index, rows, columns)
-        ctab_ref[number] = column_table
-        rtab_ref[number] = row_table
-
-    def picked(number, parts):
-        return pick(parts, ctab_ref[number], rtab_ref[number])
-
-    def placed(number, amount):
-        return place(amount, ctab_ref[number], rtab_ref[number], rows)
-
-    def parts_of(ref, s=None):
-        return [
-            split(stacked(ref[i] if s is None else ref[s, i], rows)) for i in range(2)
-        ]
-
-    store_tables(1, src_ref[1:2, :])
-    parts_1 = parts_of(u_ref, 1)
-    points_1 = picked(1, parts_1)
+        ctab_ref[section, :, half * slots : (half + 1) * slots] = column_table
+        rtab_ref[section, :, half * slots : (half + 1) * slots] = row_table
+
+    def picked(section, half, parts):
+        lanes = slice(half * slots, (half + 1) * slots)
+        return pick(parts, ctab_ref[section, :, lanes], rtab_ref[section, :, lanes])
+
+    def picked_both(section, parts):
+        both = pick(parts, ctab_ref[section], rtab_ref[section])
+        return [x[:, :slots] for x in both], [x[:, slots:] for x in both]
+
+    def split_parts(grids):
+        pairs = [split(stacked(grid, rows)) for grid in grids]
+        return jnp.concatenate([pairs[0][0], pairs[1][0], pairs[0][1], pairs[1][1]], axis=0)
+
+    def parts_of(section):
+        return split_parts([u_ref[section, i] for i in range(2)])
+
+    store_tables(1, 0, src_ref[1:2, :])
+    store_tables(1, 1, tgt_ref[0:1, :])
+    points_1, ends_0 = picked_both(1, parts_of(1))
     slot_send[0, 0:1, :] = tgt_ref[1:2, :].astype(F32)
     slot_send[0, 1:2, :] = weights[1]
     slot_send[0, 2:3, :] = points_1[0]
@@ -239,23 +254,18 @@
     ]
     slots_in, down_in, up_in = copies
 
-    store_tables(0, src_ref[0:1, :])
-    store_tables(2, tgt_ref[0:1, :])
-    parts_0 = parts_of(u_ref, 0)
-    points_0 = picked(0, parts_0)
-    ends_0 = picked(2, parts_1)
+    store_tables(0, 0, src_ref[0:1, :])
+    points_0 = picked(0, 0, parts_of(0))
     loads[5].wait()
     first_sec = sec == 0
 
     def slab_parts():
-        return [
-            split(stacked(jnp.where(first_sec, a_ref[i], u_ref[0, i]), rows)) for i in range(2)
-        ]
+        return split_parts([jnp.where(first_sec, a_ref[i], u_ref[0, i]) for i in range(2)])
 
     slots_in.wait_recv()
-    store_tables(3, slot_recv[0, 0:1, :].astype(jnp.int32))
+    store_tables(0, 1, slot_recv[0, 0:1, :].astype(jnp.int32))
     weight_in = slot_recv[0, 1:2, :] * jnp.where(first_sec, 0.0, 1.0)
-    ends_in = picked(3, slab_parts())
+    ends_in = picked(0, 1, slab_parts())
     points_in = [slot_recv[0, 2:3, :], slot_recv[0, 3:4, :]]
     points_send[0, 0:1, :] = ends_in[0]
     points_send[0, 1:2, :] = ends_in[1]
@@ -318,13 +328,26 @@
 
         match_0 = [weights[0] * (ends_0[i] - points_0[i]) for i in range(2)]
         match_in = [weight_in * (ends_in[i] - points_in[i]) for i in range(2)]
+        added = place(
+            [jnp.concatenate([match_0[i], -match_in[i]], axis=1) for i in range(2)],
+            ctab_ref[0],
+            rtab_ref[0],
+            rows,
+        )
+        for i in range(2):
+            force_ref[0, i] = force_ref[0, i] + added[i]
         points.wait_recv()
-        sums = []
+        match_1 = [
+            weights[1] * (points_recv[iteration, i : i + 1, :] - points_1[i]) for i in range(2)
+        ]
+        added = place(
+            [jnp.concatenate([match_1[i], -match_0[i]], axis=1) for i in range(2)],
+            ctab_ref[1],
+            rtab_ref[1],
+            rows,
+        )
         for i in range(2):
-            found = points_recv[iteration, i : i + 1, :]
-            match_1 = weights[1] * (found - points_1[i])
-            force_ref[0, i] = force_ref[0, i] + placed(0, match_0[i]) - placed(3, match_in[i])
-            force_ref[1, i] = force_ref[1, i] + placed(1, match_1) - placed(2, match_0[i])
+            force_ref[1, i] = force_ref[1, i] + added[i]
 
         for s in range(sections):
             force_sq, speed_sq = 0.0, 0.0
@@ -362,6 +385,16 @@
             edge_up = near(5, edge_send.at[1], edge_recv.at[1], (above, sec))
             copies += [edge_down, edge_up]
 
+        if iteration == ITERS - 1:
+            stores = [
+                pltpu.make_async_copy(source, target, out_sem.at[i])
+                for i, (source, target) in enumerate(
+                    [(mid_ref, out_mid), (force_ref, out_force), (u_ref, out_u)]
+                )
+            ]
+            for store in stores:
+                store.start()
+
         total = sums_send[iteration, 0:4, :]
         for peer in peers:
             peer.wait_recv()
@@ -371,6 +404,14 @@
         ratio = jnp.sqrt(total[2:4]) / jnp.sqrt(total[0:2] + epsilon)
         keep = [(1 - rst[iteration, s]).astype(F32) for s in range(sections)]
 
+        if iteration == ITERS - 1:
+            for s in range(sections):
+                push_ref[s : s + 1, :] = jnp.broadcast_to(
+                    mixing * ratio[s : s + 1, :] * keep[s], (1, columns)
+                )
+                decay_ref[s : s + 1, :] = jnp.full((1, columns), (1.0 - mixing) * keep[s], F32)
+            break
+
         for s in range(sections):
             push = mixing * ratio[s : s + 1, :]
             for i in range(2):
@@ -379,18 +420,16 @@
                 u_ref[s, i] = u_ref[s, i] + max_step * jnp.tanh(time_step / max_step * speed)
 
         if iteration < ITERS - 1:
-            parts_1 = parts_of(u_ref, 1)
-            points_1 = picked(1, parts_1)
+            points_1, ends_0 = picked_both(1, parts_of(1))
             slot_send[1, 0:1, :] = points_1[0]
             slot_send[1, 1:2, :] = points_1[1]
             slots_in = near(6, slot_send.at[1], slot_recv.at[1], (tile, after))
-            ends_in = picked(3, slab_parts())
+            ends_in = picked(0, 1, slab_parts())
             points_send[1, 0:1, :] = ends_in[0]
             points_send[1, 1:2, :] = ends_in[1]
             points = near(7, points_send.at[1], points_recv.at[1], (tile, before))
             copies += [slots_in, points]
-            points_0 = picked(0, parts_of(u_ref, 0))
-            ends_0 = picked(2, parts_1)
+            points_0 = picked(0, 0, parts_of(0))
 
             half = lax.broadcasted_iota(jnp.int32, (4, columns), 0) < 2
             ratio_rows = jnp.where(half, mixing * ratio[0:1, :], mixing * ratio[1:2, :])
@@ -407,12 +446,9 @@
             slots_in.wait_recv()
             points_in = [slot_recv[1, 0:1, :], slot_recv[1, 1:2, :]]
 
-    stores = [
-        pltpu.make_async_copy(v_ref, out_v, out_sem.at[0]),
-        pltpu.make_async_copy(u_ref, out_u, out_sem.at[1]),
-    ]
-    for store in stores:
-        store.start()
+    for i, (source, target) in enumerate([(push_ref, out_push), (decay_ref, out_decay)]):
+        stores.append(pltpu.make_async_copy(source, target, out_sem.at[3 + i]))
+        stores[-1].start()
     for copy in copies:
         copy.wait_send()
     for store in stores:
@@ -428,12 +464,14 @@
     anywhere = pl.BlockSpec(memory_space=pl.ANY)
     scalars = pl.BlockSpec(memory_space=pltpu.SMEM)
     field = jax.ShapeDtypeStruct(displacement.shape, F32)
+    gain = jax.ShapeDtypeStruct((sections, columns), F32)
     vmem = pltpu.VMEM
-    return pl.pallas_call(
+    counts = arguments[7].T
+    middle, force, current, push, decay = pl.pallas_call(
         functools.partial(kernel, n_tile, n_sec),
-        out_shape=(field, field),
-        in_specs=[anywhere] * 7 + [scalars] * 2,
-        out_specs=(anywhere, anywhere),
+        out_shape=(field, field, field, gain, gain),
+        in_specs=[pl.BlockSpec(memory_space=pltpu.HBM)] * 7 + [scalars] * 2,
+        out_specs=(anywhere,) * 5,
         scratch_shapes=[
             vmem(displacement.shape, F32),
             vmem(velocity.shape, F32),
@@ -445,10 +483,12 @@
             vmem(stiffness.shape, F32),
             vmem(displacement.shape, F32),
             vmem(displacement.shape, F32),
-            vmem((4, 128, slots), BF16),
-            vmem((4, pieces * rows, slots), F32),
+            vmem((2, 128, 2 * slots), BF16),
+            vmem((2, pieces * rows, 2 * slots), F32),
+            vmem((sections, columns), F32),
+            vmem((sections, columns), F32),
             dma((7,)),
-            dma((2,)),
+            dma((5,)),
             vmem((16, columns), F32),
             vmem((8, columns), F32),
             vmem((16, columns), F32),
@@ -472,7 +512,9 @@
         cost_estimate=pl.CostEstimate(
             flops=40_000_000, bytes_accessed=1_500_000, transcendentals=1_000_000
         ),
-    )(*arguments)
+    )(*arguments[:7], counts, arguments[8])
+    speed = decay[:, None, None, :] * middle + push[:, None, None, :] * force
+    return current + max_step * jnp.tanh(time_step * speed / max_step), speed
 
 
 def solution(mesh):

time: 28.7 us -> 27.5 us (0.958)
  local copies, waits for them, and re-layouts: 3.72 us -> 0.69 us
  other arithmetic: 0 us -> 1.96 us
    unnamed x5 -> x2, local copies, waits for them, and re-layouts: 3.72 us -> 0.69 us
    add x0 -> x1, other arithmetic: none -> 1.96 us  [local(): return (current + max_step * jnp.tanh(time_step * speed / max_step), speed)]
where the time goes in v2:
time: 27.5 us; the launch traced here: 27.2 us
  Pallas kernels  23.9 us (87%)
  other arithmetic  1.96 us (7%)
  local copies, waits for them, and re-layouts  0.69 us (3%)
  between operations  0.65 us (2%)
    pallas_call x1, Pallas kernels, local(): pl.pallas_call(functools.partial(kernel, n_tile, n_sec), out_shape=(field...  23.9 us
    add x1, other arithmetic, local(): return (current + max_step * jnp.tanh(time_step * speed / max_step), speed)  1.96 us
    unnamed x2, local copies, waits for them, and re-layouts  0.69 us

profile of v2, /device:TPU:0, one launch (start us, length us, event | category | flops | bytes accessed | tf_op | source)
XLA Modules:
  0.0 27.2 jit_solution(11358704426884254653)
XLA Ops:
  0.6 23.9 %shard_map.104 = (f32[2,2,16,1024]{3,2,1,0:T(8,128)}, f32[2,2,16,1024]{3,2,1,0:T(8,128)}, f32[2,2,16,1024]{3,2,1,0:T(8,128)}, f32[2,1024]{1,0:T(2,128)}, f32[2,1024]{1,0:T(2,128)}) custom-call(f32[2,2,16,1024]{3,2,1,0:T(8,128)} %u_hbm.1, f32[2,2,16,1024]{3,2,1,0:T(8,128)} %v_hbm.1, bf16[2,4,16,1024]{3,2,1,0:T(8,128)(2,1)} %k_hbm.1, f32[2,16,1024]{2,1,0:T(8,128)} %a_hbm.1, ...), custom_call_target="tpu_custom_call" | custom-call | flops 40000000 | bytes 1500000 | tf_op jit(solution)/shard_map/pallas_call | solution.py:470
  24.6 0.0 copy-start
  24.6 0.7 %copy-done = f32[2,1024]{1,0:T(2,128)S(1)} copy-done((f32[2,1024]{1,0:T(2,128)S(1)}, f32[2,1024]{1,0:T(2,128)}, u32[]{:S(2)}) %copy-start) | copy-done | bytes 8216
  25.3 2.0 %multiply_add_fusion = (f32[2,2,16,1024]{3,2,1,0:T(8,128)}, f32[2,2,16,1024]{3,2,1,0:T(8,128)}) fusion(f32[2,2,16,1024]{3,2,1,0:T(8,128)} %get-tuple-element.7, f32[2,2,16,1024]{3,2,1,0:T(8,128)} %get-tuple-element.11, f32[2,1024]{1,0:T(2,128)S(1)} %copy-done, f32[2,2,16,1024]{3,2,1,0:T(8,128)} %get-tuple-element.9, f32[2,1024]{1,0:T(2,128)} %get-tuple-element.8), kind=kLoop, calls=%fused_computation | loop fusion | flops 393216 | bytes 1327104 | tf_op jit(solution)/shard_map/add | solution.py:517
Async XLA Ops:
  24.6 0.7 %copy-start = (f32[2,1024]{1,0:T(2,128)S(1)}, f32[2,1024]{1,0:T(2,128)}, u32[]{:S(2)}) copy-start(f32[2,1024]{1,0:T(2,128)} %get-tuple-element.10) | copy-start | bytes 24580

commit v3 on v2

--- a/solution.py
+++ b/solution.py
@@ -17,11 +17,6 @@
 MESH = pl.DeviceIdType.MESH
 F32 = jnp.float32
 BF16 = jnp.bfloat16
-
-
-def split(value):
-    high = value.astype(BF16)
-    return high, (value - high.astype(F32)).astype(BF16)
 
 
 def from_left(values):
@@ -76,21 +71,19 @@
     nodes = row_table.shape[0]
     result = []
     for i in range(2):
-        both = found[i * nodes : (i + 1) * nodes] + found[(2 + i) * nodes : (3 + i) * nodes]
+        both = found[i * nodes : (i + 1) * nodes]
         result.append(jnp.sum(both * row_table, axis=0, keepdims=True))
     return result
 
 
 def place(amounts, column_table, row_table, rows):
-    highs = [amount.astype(BF16).astype(F32) for amount in amounts]
-    lows = [amount - high for amount, high in zip(amounts, highs)]
-    spread = jnp.concatenate([(x * row_table).astype(BF16) for x in highs + lows], axis=0)
+    spread = jnp.concatenate([(x * row_table).astype(BF16) for x in amounts], axis=0)
     out = lax.dot_general(
         spread, column_table, (((1,), (1,)), ((), ())), preferred_element_type=F32
     )
     nodes = row_table.shape[0]
     return [
-        unstacked(out[i * nodes : (i + 1) * nodes] + out[(2 + i) * nodes : (3 + i) * nodes], rows)
+        unstacked(out[i * nodes : (i + 1) * nodes], rows)
         for i in range(2)
     ]
 
@@ -231,12 +224,11 @@
         both = pick(parts, ctab_ref[section], rtab_ref[section])
         return [x[:, :slots] for x in both], [x[:, slots:] for x in both]
 
-    def split_parts(grids):
-        pairs = [split(stacked(grid, rows)) for grid in grids]
-        return jnp.concatenate([pairs[0][0], pairs[1][0], pairs[0][1], pairs[1][1]], axis=0)
+    def stacked_parts(grids):
+        return jnp.concatenate([stacked(grid, rows).astype(BF16) for grid in grids], axis=0)
 
     def parts_of(section):
-        return split_parts([u_ref[section, i] for i in range(2)])
+        return stacked_parts([u_ref[section, i] for i in range(2)])
 
     store_tables(1, 0, src_ref[1:2, :])
     store_tables(1, 1, tgt_ref[0:1, :])
@@ -260,7 +252,7 @@
     first_sec = sec == 0
 
     def slab_parts():
-        return split_parts([jnp.where(first_sec, a_ref[i], u_ref[0, i]) for i in range(2)])
+        return stacked_parts([jnp.where(first_sec, a_ref[i], u_ref[0, i]) for i in range(2)])
 
     slots_in.wait_recv()
     store_tables(0, 1, slot_recv[0, 0:1, :].astype(jnp.int32))

time: 27.5 us -> 27.2 us (0.989)
  Pallas kernels: 23.9 us -> 23.6 us
    pallas_call x1, Pallas kernels: 23.9 us -> 23.6 us  [local(): pl.pallas_call(functools.partial(kernel, n_tile, n_sec), out_shape=(field...]
where the time goes in v3:
time: 27.2 us; the launch traced here: 26.9 us
  Pallas kernels  23.6 us (87%)
  other arithmetic  1.96 us (7%)
  local copies, waits for them, and re-layouts  0.69 us (3%)
  between operations  0.65 us (2%)
    pallas_call x1, Pallas kernels, local(): pl.pallas_call(functools.partial(kernel, n_tile, n_sec), out_shape=(field...  23.6 us
    add x1, other arithmetic, local(): return (current + max_step * jnp.tanh(time_step * speed / max_step), speed)  1.96 us
    unnamed x2, local copies, waits for them, and re-layouts  0.69 us

profile of v3, /device:TPU:0, one launch (start us, length us, event | category | flops | bytes accessed | tf_op | source)
XLA Modules:
  0.0 26.9 jit_solution(13685602673881739701)
XLA Ops:
  0.6 23.6 %shard_map.104 = (f32[2,2,16,1024]{3,2,1,0:T(8,128)}, f32[2,2,16,1024]{3,2,1,0:T(8,128)}, f32[2,2,16,1024]{3,2,1,0:T(8,128)}, f32[2,1024]{1,0:T(2,128)}, f32[2,1024]{1,0:T(2,128)}) custom-call(f32[2,2,16,1024]{3,2,1,0:T(8,128)} %u_hbm.1, f32[2,2,16,1024]{3,2,1,0:T(8,128)} %v_hbm.1, bf16[2,4,16,1024]{3,2,1,0:T(8,128)(2,1)} %k_hbm.1, f32[2,16,1024]{2,1,0:T(8,128)} %a_hbm.1, ...), custom_call_target="tpu_custom_call" | custom-call | flops 40000000 | bytes 1500000 | tf_op jit(solution)/shard_map/pallas_call | solution.py:462
  24.3 0.0 copy-start
  24.3 0.7 %copy-done = f32[2,1024]{1,0:T(2,128)S(1)} copy-done((f32[2,1024]{1,0:T(2,128)S(1)}, f32[2,1024]{1,0:T(2,128)}, u32[]{:S(2)}) %copy-start) | copy-done | bytes 8216
  25.0 2.0 %multiply_add_fusion = (f32[2,2,16,1024]{3,2,1,0:T(8,128)}, f32[2,2,16,1024]{3,2,1,0:T(8,128)}) fusion(f32[2,2,16,1024]{3,2,1,0:T(8,128)} %get-tuple-element.7, f32[2,2,16,1024]{3,2,1,0:T(8,128)} %get-tuple-element.11, f32[2,1024]{1,0:T(2,128)S(1)} %copy-done, f32[2,2,16,1024]{3,2,1,0:T(8,128)} %get-tuple-element.9, f32[2,1024]{1,0:T(2,128)} %get-tuple-element.8), kind=kLoop, calls=%fused_computation | loop fusion | flops 393216 | bytes 1327104 | tf_op jit(solution)/shard_map/add | solution.py:509
Async XLA Ops:
  24.3 0.7 %copy-start = (f32[2,1024]{1,0:T(2,128)S(1)}, f32[2,1024]{1,0:T(2,128)}, u32[]{:S(2)}) copy-start(f32[2,1024]{1,0:T(2,128)} %get-tuple-element.10) | copy-start | bytes 24580
